TPU v7x, 128 devices: a whole 4x4x4 slice. The times are simulated.
128 devices in a mesh: sim: 2 (over x_hi), tm: 64 (over y, z, x_lo, core).
Axes of the slice: x: 4 (x_hi: 2, x_lo: 2; x = x_hi * 2 + x_lo), y: 4, z: 4, core: 2. Of those that a mesh axis runs over, the one named last changes fastest.
Arguments:
- strain: bfloat16 [3, 1048576], P(None, ('sim', 'tm')), parts along dimension 1, may hold values from -40 to 40, as said below
- stem_weight: bfloat16 [768, 48], replicated, may hold values from -6 to 6
- norm_gain: float32 [768], replicated, may hold values from 0.1 to 1.9
- qkv_weight: bfloat16 [768, 1152], replicated, may hold values from -3 to 3
- out_weight: bfloat16 [768, 768], replicated, may hold values from -0.21875 to 0.21875
- cotangent: bfloat16 [65536, 768], P(('sim', 'tm')), parts along dimension 0, may hold values from -6 to 6
Outputs:
- grad_qkv: float32 [1536, 1152], P(('sim', 'tm')), parts along dimension 0
- grad_out: float32 [1536, 768], P(('sim', 'tm')), parts along dimension 0
- grad_stem: float32 [1536, 48], P(('sim', 'tm')), parts along dimension 0
- grad_gain: float32 [1536], P(('sim', 'tm')), parts along dimension 0
There are 2 independent parts, one for each index of `sim`. A program takes and returns all parts, laid end to end along the dimension named above; an argument that names none is the same for every part. Nothing has to cross between parts.
Inputs may be any that keep to these rules, and one draw needn't show every extreme that they name: `strain`: strain samples of one evolution.
All inputs are finite; a program needn't handle non-finite values.
Results may differ from a plain program's by a relative error of at most 0.0065.
The roundings to bfloat16 on the way count: a program that leaves them out, or rounds other values in their place, can miss the bound.
Values may be sent and summed in bfloat16 or wider, within the bound.
No kernel may reach another device: no remote copies, remote signals or barrier semaphores. Data moves between devices by JAX's collectives and lax.ppermute only.
A program may use at most 64 MiB of HBM per device.

v0:
```python
import jax
import jax.numpy as jnp
from jax import lax
from jax.sharding import PartitionSpec as P

HEAD_SIZE = 64
STRIDE = 16


EPSILON = 1e-05


def passed_along(shard, axis, by):
    devices = lax.axis_size(axis)
    return lax.ppermute(shard, axis, [(i, (i + by) % devices) for i in range(devices)])


def embed_strain(samples, stem_weight, norm_gain):
    channels = samples.shape[0]
    blocks = samples.reshape(channels, -1, STRIDE)
    kernel = stem_weight.reshape(stem_weight.shape[0], channels, STRIDE)
    features = jnp.einsum("cts,dcs->td", blocks, kernel, preferred_element_type=jnp.float32)
    inverse_rms = lax.rsqrt(jnp.mean(features * features, axis=-1) + EPSILON)
    normed = (features * inverse_rms[:, None] * norm_gain).astype(jnp.bfloat16)
    return (features, inverse_rms, normed)


def norm_back(grad_normed, features, inverse_rms, norm_gain, samples):
    scaled = grad_normed * norm_gain
    inner = jnp.mean(scaled * features, axis=-1)
    grad_features = inverse_rms[:, None] * scaled - features * (inverse_rms**3 * inner)[:, None]
    channels = samples.shape[0]
    blocks = samples.astype(jnp.float32).reshape(channels, -1, STRIDE)
    stem_term = jnp.einsum("td,cts->dcs", grad_features, blocks, precision=lax.Precision.HIGHEST)
    stem_term = stem_term.reshape(grad_features.shape[1], -1)
    gain_term = jnp.sum(grad_normed * features * inverse_rms[:, None], axis=0)
    return (stem_term, gain_term)


def attend(query_matrix, key_rows, value_rows, attention_gradient):
    row_count = query_matrix.shape[0]
    group_count = key_rows.shape[1] // HEAD_SIZE
    shared_portion = query_matrix.shape[1] // HEAD_SIZE // group_count
    outputs = [[], [], [], [], [], []]
    for query_group in range(group_count):
        query_cols = slice(
            query_group * shared_portion * HEAD_SIZE, (query_group + 1) * shared_portion * HEAD_SIZE
        )
        head_cols = slice(query_group * HEAD_SIZE, (query_group + 1) * HEAD_SIZE)
        query_heads = query_matrix[:, query_cols].reshape(row_count, shared_portion, HEAD_SIZE)
        key_head = key_rows[:, head_cols]
        value_head = value_rows[:, head_cols]
        grad_heads = attention_gradient[:, query_cols].reshape(row_count, shared_portion, HEAD_SIZE)
        scores = jnp.einsum(
            "tjd,sd->jts", query_heads, key_head, preferred_element_type=jnp.float32
        ) * HEAD_SIZE ** (-0.5)
        row_max = jnp.max(scores, axis=-1, keepdims=True)
        weights = jnp.exp(scores - row_max)
        probs = weights / jnp.sum(weights, axis=-1, keepdims=True)
        probs_low = probs.astype(jnp.bfloat16)
        mixed = jnp.einsum("jts,sd->tjd", probs_low, value_head, preferred_element_type=jnp.float32)
        grad_probs = jnp.einsum(
            "tjd,sd->jts", grad_heads, value_head, preferred_element_type=jnp.float32
        )
        delta = jnp.sum(probs * grad_probs, axis=-1, keepdims=True)
        grad_scores = (probs * (grad_probs - delta)).astype(jnp.bfloat16)
        grad_query = jnp.einsum(
            "jts,sd->tjd", grad_scores, key_head, preferred_element_type=jnp.float32
        ) * HEAD_SIZE ** (-0.5)
        grad_keys = jnp.einsum(
            "jts,tjd->sd", grad_scores, query_heads, preferred_element_type=jnp.float32
        ) * HEAD_SIZE ** (-0.5)
        grad_values = jnp.einsum(
            "jts,tjd->sd", probs_low, grad_heads, preferred_element_type=jnp.float32
        )
        outputs[0].append(mixed.astype(jnp.bfloat16).reshape(row_count, -1))
        outputs[1].append(grad_query.astype(jnp.bfloat16).reshape(row_count, -1))
        outputs[2].append(grad_keys[:row_count].astype(jnp.bfloat16))
        outputs[3].append(grad_keys[row_count:].astype(jnp.bfloat16))
        outputs[4].append(grad_values[:row_count].astype(jnp.bfloat16))
        outputs[5].append(grad_values[row_count:].astype(jnp.bfloat16))
    return tuple((jnp.concatenate(pieces, axis=1) for pieces in outputs))


def contract_rows(left, right):
    return lax.dot_general(
        left, right, (((0,), (0,)), ((), ())), preferred_element_type=jnp.float32
    )


def contract_cols(left, right):
    return lax.dot_general(
        left, right, (((1,), (1,)), ((), ())), preferred_element_type=jnp.float32
    )


def local(strain, stem_weight, norm_gain, qkv_weight, out_weight, cotangent):
    features, inverse_rms, normed = embed_strain(strain, stem_weight, norm_gain)
    projected_rows = jnp.dot(normed, qkv_weight, preferred_element_type=jnp.float32).astype(
        jnp.bfloat16
    )
    attention_span = out_weight.shape[1]
    own_pairs = projected_rows[:, attention_span:]
    kv_weight = qkv_weight[:, attention_span:]
    prev_pairs = passed_along(own_pairs, "tm", 1)
    key_width = own_pairs.shape[1] // 2
    key_rows = jnp.concatenate([prev_pairs[:, :key_width], own_pairs[:, :key_width]], axis=0)
    value_rows = jnp.concatenate([prev_pairs[:, key_width:], own_pairs[:, key_width:]], axis=0)
    attention_gradient = jnp.dot(cotangent, out_weight, preferred_element_type=jnp.float32).astype(
        jnp.bfloat16
    )
    mixed, grad_query, key_prev, key_mine, value_prev, value_mine = attend(
        projected_rows[:, :attention_span], key_rows, value_rows, attention_gradient
    )
    own_grads = jnp.concatenate([grad_query, key_mine, value_mine], axis=1)
    sent_grads = jnp.concatenate([key_prev, value_prev], axis=1)
    grad_normed = contract_cols(own_grads, qkv_weight)
    returned = passed_along(sent_grads, "tm", -1)
    grad_normed = grad_normed + contract_cols(returned, kv_weight)
    stem_term, gain_term = norm_back(grad_normed, features, inverse_rms, norm_gain, strain)
    result = contract_rows(normed, own_grads)
    grad_qkv = lax.psum_scatter(
        result.at[:, attention_span:].add(contract_rows(normed, returned)),
        "tm",
        scatter_dimension=0,
        tiled=True,
    )
    grad_out = lax.psum_scatter(
        contract_rows(cotangent, mixed), "tm", scatter_dimension=0, tiled=True
    )
    grad_stem, grad_gain = (
        lax.psum_scatter(stem_term, "tm", scatter_dimension=0, tiled=True),
        lax.psum_scatter(gain_term, "tm", scatter_dimension=0, tiled=True),
    )
    return (grad_qkv, grad_out, grad_stem, grad_gain)


def solution(mesh):
    in_specs = (P(None, ("sim", "tm")), P(), P(), P(), P(), P(("sim", "tm"), None))
    out_specs = (
        P(("sim", "tm"), None),
        P(("sim", "tm"), None),
        P(("sim", "tm"), None),
        P(("sim", "tm")),
    )
    return jax.shard_map(local, mesh=mesh, in_specs=in_specs, out_specs=out_specs, check_vma=False)
```

profile of v0, /device:TPU:1, one launch (start us, length us, event | category | flops | bytes accessed | tf_op | source)
XLA Modules:
  0.0 650.5 jit_solution(4385943727991690432)
XLA Ops:
  14.0 2.6 collective-permute-start
  29.0 6.8 %fusion.158 = (f32[4,512]{1,0:T(4,128)S(1)}, f32[4,512,1024]{1,2,0:T(8,128)}) fusion(bf16[512,4,64]{0,2,1:T(8,128)(2,1)} %bitcast.248, bf16[512,192]{1,0:T(8,128)(2,1)S(1)} %get-tuple-element.42, bf16[512,192]{1,0:T(8,128)(2,1)S(1)} %get-tuple-element.37), kind=kOutput, calls=%fused_computation.167 | convolution fusion | flops 274990080 | bytes 9052160 | tf_op jit(solution)/shard_map/sub | solution.py:58
  35.8 5.6 fusion.89
  44.7 2.6 fusion.17
  50.9 4.9 fusion.163
  55.8 5.3 fusion.59
  61.8 2.1 fusion.86
  65.2 2.4 fusion.12
  71.3 5.0 fusion.168
  76.3 4.5 fusion.62
  82.2 2.1 fusion.83
  85.5 2.4 fusion.7
  91.6 2.3 convolution_bitcast_fusion
  102.2 2.7 fusion.174
  105.0 3.0 fusion.173
  111.0 2.4 fusion.49
  113.4 3.0 fusion.55
  116.5 170.7 %fusion.152 = (f32[16,1152]{1,0:T(8,128)S(1)}, f32[16,48]{1,0:T(8,128)S(1)}) fusion(f32[768,1152]{1,0:T(8,128)} %fusion.55, f32[768,48]{1,0:T(8,128)} %fusion.49), kind=kCustom, calls=%all-reduce-scatter.2 | all-reduce-scatter fusion | flops 1228801 | bytes 3763712
  292.7 7.5 %collective-permute-start.33 = (f32[12,48]{1,0:T(8,128)S(1)}, f32[12,48]{1,0:T(8,128)S(1)}, u32[]{:S(2)}, u32[]{:S(2)}) collective-permute-start(f32[12,48]{1,0:T(8,128)S(1)} %slice.191), channel_id=1, source_target_pairs={{0,16},{1,17},{2,18},{3,19},{4,20},{5,21},{6,22},{7,23},{8,24},{9,... | collective-permute-start | bytes 6920
  303.5 14.0 %collective-permute-start.27 = (f32[16,48]{1,0:T(8,128)S(1)}, f32[16,48]{1,0:T(8,128)S(1)}, u32[]{:S(2)}, u32[]{:S(2)}) collective-permute-start(f32[16,48]{1,0:T(8,128)S(1)} %get-tuple-element.33), channel_id=1, source_target_pairs={{0,10},{1,11},{2,12},{3,13},{4,14},{5,15},{6,16},{7,17},{8,18},{9,... | collective-permute-start | bytes 9224
  317.6 2.2 collective-permute-start.26
  319.8 4.5 collective-permute-start.25
  327.6 5.3 collective-permute-start.22
  334.2 2.6 collective-permute-start.20
  336.8 2.5 collective-permute-start.19
  339.3 3.6 collective-permute-start.18
  344.2 3.0 collective-permute-start.15
  351.6 2.9 collective-permute-start.11
  354.6 4.0 collective-permute-start.10
  365.8 139.2 %all-reduce.3 = f32[768]{0:T(1024)S(1)} all-reduce(f32[768]{0:T(1024)S(1)} %get-tuple-element.28), channel_id=5, replica_groups=mesh['sim'=2,'tm'=64] {'tm'}, use_global_device_ids=true, to_apply=%region_15.0.clone | all-reduce | flops 768 | bytes 6144
  516.0 3.9 concatenate.22
  520.5 120.6 %all-reduce.9.cloned.1.call-done = f32[768,768]{0,1:T(8,128)} async-done(((f32[768,768]{0,1:T(8,128)}), f32[768,768]{0,1:T(8,128)}) %all-reduce.9.cloned.1.call-update) | async-done | bytes 2359312
  (158 shorter events, 87.8 us)
Async XLA Ops:
  7.2 633.9 %all-reduce.9.cloned.1.call-start = ((), (), s32[]{:S(2)}) async-start(), calls=%async_computation | async-start | bytes 4718592
  14.0 13.1 %collective-permute-start = (bf16[512,384]{1,0:T(8,128)(2,1)}, bf16[512,384]{1,0:T(8,128)(2,1)}, u32[]{:S(2)}, u32[]{:S(2)}) collective-permute-start(bf16[512,384]{1,0:T(8,128)(2,1)} %slice.158), channel_id=1, source_target_pairs={{0,1},{1,2},{2,3},{3,4},{4,5},{5,6},{6,7},{7,8},{8,9},{9,10},{10,1... | collective-permute-start | bytes 1179656 | tf_op jit(solution)/shard_map/ppermute | solution.py:15
  101.1 7.9 %collective-permute-start.1 = (bf16[512,384]{0,1:T(8,128)(2,1)S(1)}, bf16[512,384]{0,1:T(8,128)(2,1)S(1)}, u32[]{:S(2)}, u32[]{:S(2)}) collective-permute-start(bf16[512,384]{0,1:T(8,128)(2,1)S(1)} %get-tuple-element.44), channel_id=1, source_target_pairs={{0,63},{1,0},{2,1},{3,2},{4,3},{5,4},{6,5},{7,6},{8,7},{9,8},{10,9... | collective-permute-start | bytes 1179656 | tf_op jit(solution)/shard_map/ppermute | solution.py:15
  287.2 63.1 %collective-permute-start.17 = (f32[12,1152]{1,0:T(8,128)S(1)}, f32[12,1152]{1,0:T(8,128)S(1)}, u32[]{:S(2)}, u32[]{:S(2)}) collective-permute-start(f32[12,1152]{1,0:T(8,128)S(1)} %slice.190), channel_id=1, source_target_pairs={{0,16},{1,17},{2,18},{3,19},{4,20},{5,21},{6,22},{7,23},{8,24},{9,... | collective-permute-start | bytes 165896
  288.5 13.7 %collective-permute-start.32 = (f32[16,48]{1,0:T(8,128)S(1)}, f32[16,48]{1,0:T(8,128)S(1)}, u32[]{:S(2)}, u32[]{:S(2)}) collective-permute-start(f32[16,48]{1,0:T(8,128)S(1)} %get-tuple-element.33), channel_id=1, source_target_pairs={{0,15},{1,16},{2,17},{3,18},{4,19},{5,20},{6,21},{7,22},{8,23},{9,... | collective-permute-start | bytes 9224
  289.8 13.7 %collective-permute-start.31 = (f32[16,48]{1,0:T(8,128)S(1)}, f32[16,48]{1,0:T(8,128)S(1)}, u32[]{:S(2)}, u32[]{:S(2)}) collective-permute-start(f32[16,48]{1,0:T(8,128)S(1)} %get-tuple-element.33), channel_id=1, source_target_pairs={{0,14},{1,15},{2,16},{3,17},{4,18},{5,19},{6,20},{7,21},{8,22},{9,... | collective-permute-start | bytes 9224
  291.3 26.2 %collective-permute-start.30 = (f32[16,48]{1,0:T(8,128)S(1)}, f32[16,48]{1,0:T(8,128)S(1)}, u32[]{:S(2)}, u32[]{:S(2)}) collective-permute-start(f32[16,48]{1,0:T(8,128)S(1)} %get-tuple-element.33), channel_id=1, source_target_pairs={{0,13},{1,14},{2,15},{3,16},{4,17},{5,18},{6,19},{7,20},{8,21},{9,... | collective-permute-start | bytes 9224
  292.7 8.3 %collective-permute-start.33 = (f32[12,48]{1,0:T(8,128)S(1)}, f32[12,48]{1,0:T(8,128)S(1)}, u32[]{:S(2)}, u32[]{:S(2)}) collective-permute-start(f32[12,48]{1,0:T(8,128)S(1)} %slice.191), channel_id=1, source_target_pairs={{0,16},{1,17},{2,18},{3,19},{4,20},{5,21},{6,22},{7,23},{8,24},{9,... | collective-permute-start | bytes 6920
  300.9 18.9 %collective-permute-start.29 = (f32[16,48]{1,0:T(8,128)S(1)}, f32[16,48]{1,0:T(8,128)S(1)}, u32[]{:S(2)}, u32[]{:S(2)}) collective-permute-start(f32[16,48]{1,0:T(8,128)S(1)} %get-tuple-element.33), channel_id=1, source_target_pairs={{0,12},{1,13},{2,14},{3,15},{4,16},{5,17},{6,18},{7,19},{8,20},{9,... | collective-permute-start | bytes 9224
  302.2 22.1 %collective-permute-start.28 = (f32[16,48]{1,0:T(8,128)S(1)}, f32[16,48]{1,0:T(8,128)S(1)}, u32[]{:S(2)}, u32[]{:S(2)}) collective-permute-start(f32[16,48]{1,0:T(8,128)S(1)} %get-tuple-element.33), channel_id=1, source_target_pairs={{0,11},{1,12},{2,13},{3,14},{4,15},{5,16},{6,17},{7,18},{8,19},{9,... | collective-permute-start | bytes 9224
  303.5 22.7 %collective-permute-start.27 = (f32[16,48]{1,0:T(8,128)S(1)}, f32[16,48]{1,0:T(8,128)S(1)}, u32[]{:S(2)}, u32[]{:S(2)}) collective-permute-start(f32[16,48]{1,0:T(8,128)S(1)} %get-tuple-element.33), channel_id=1, source_target_pairs={{0,10},{1,11},{2,12},{3,13},{4,14},{5,15},{6,16},{7,17},{8,18},{9,... | collective-permute-start | bytes 9224
  317.6 10.0 %collective-permute-start.26 = (f32[16,48]{1,0:T(8,128)S(1)}, f32[16,48]{1,0:T(8,128)S(1)}, u32[]{:S(2)}, u32[]{:S(2)}) collective-permute-start(f32[16,48]{1,0:T(8,128)S(1)} %get-tuple-element.33), channel_id=1, source_target_pairs={{0,9},{1,10},{2,11},{3,12},{4,13},{5,14},{6,15},{7,16},{8,17},{9,1... | collective-permute-start | bytes 9224
  319.8 13.0 %collective-permute-start.25 = (f32[16,48]{1,0:T(8,128)S(1)}, f32[16,48]{1,0:T(8,128)S(1)}, u32[]{:S(2)}, u32[]{:S(2)}) collective-permute-start(f32[16,48]{1,0:T(8,128)S(1)} %get-tuple-element.33), channel_id=1, source_target_pairs={{0,8},{1,9},{2,10},{3,11},{4,12},{5,13},{6,14},{7,15},{8,16},{9,17... | collective-permute-start | bytes 9224
  324.3 9.8 %collective-permute-start.24 = (f32[16,48]{1,0:T(8,128)S(1)}, f32[16,48]{1,0:T(8,128)S(1)}, u32[]{:S(2)}, u32[]{:S(2)}) collective-permute-start(f32[16,48]{1,0:T(8,128)S(1)} %get-tuple-element.33), channel_id=1, source_target_pairs={{0,7},{1,8},{2,9},{3,10},{4,11},{5,12},{6,13},{7,14},{8,15},{9,16}... | collective-permute-start | bytes 9224
  326.3 10.5 %collective-permute-start.23 = (f32[16,48]{1,0:T(8,128)S(1)}, f32[16,48]{1,0:T(8,128)S(1)}, u32[]{:S(2)}, u32[]{:S(2)}) collective-permute-start(f32[16,48]{1,0:T(8,128)S(1)} %get-tuple-element.33), channel_id=1, source_target_pairs={{0,6},{1,7},{2,8},{3,9},{4,10},{5,11},{6,12},{7,13},{8,14},{9,15},... | collective-permute-start | bytes 9224
  327.6 11.7 %collective-permute-start.22 = (f32[16,48]{1,0:T(8,128)S(1)}, f32[16,48]{1,0:T(8,128)S(1)}, u32[]{:S(2)}, u32[]{:S(2)}) collective-permute-start(f32[16,48]{1,0:T(8,128)S(1)} %get-tuple-element.33), channel_id=1, source_target_pairs={{0,5},{1,6},{2,7},{3,8},{4,9},{5,10},{6,11},{7,12},{8,13},{9,14},{... | collective-permute-start | bytes 9224
  332.9 10.0 %collective-permute-start.21 = (f32[16,48]{1,0:T(8,128)S(1)}, f32[16,48]{1,0:T(8,128)S(1)}, u32[]{:S(2)}, u32[]{:S(2)}) collective-permute-start(f32[16,48]{1,0:T(8,128)S(1)} %get-tuple-element.33), channel_id=1, source_target_pairs={{0,4},{1,5},{2,6},{3,7},{4,8},{5,9},{6,10},{7,11},{8,12},{9,13},{1... | collective-permute-start | bytes 9224
  334.2 10.0 %collective-permute-start.20 = (f32[16,48]{1,0:T(8,128)S(1)}, f32[16,48]{1,0:T(8,128)S(1)}, u32[]{:S(2)}, u32[]{:S(2)}) collective-permute-start(f32[16,48]{1,0:T(8,128)S(1)} %get-tuple-element.33), channel_id=1, source_target_pairs={{0,3},{1,4},{2,5},{3,6},{4,7},{5,8},{6,9},{7,10},{8,11},{9,12},{10... | collective-permute-start | bytes 9224
  336.8 10.4 %collective-permute-start.19 = (f32[16,48]{1,0:T(8,128)S(1)}, f32[16,48]{1,0:T(8,128)S(1)}, u32[]{:S(2)}, u32[]{:S(2)}) collective-permute-start(f32[16,48]{1,0:T(8,128)S(1)} %get-tuple-element.33), channel_id=1, source_target_pairs={{0,2},{1,3},{2,4},{3,5},{4,6},{5,7},{6,8},{7,9},{8,10},{9,11},{10,... | collective-permute-start | bytes 9224
  339.3 9.5 %collective-permute-start.18 = (f32[16,48]{1,0:T(8,128)S(1)}, f32[16,48]{1,0:T(8,128)S(1)}, u32[]{:S(2)}, u32[]{:S(2)}) collective-permute-start(f32[16,48]{1,0:T(8,128)S(1)} %get-tuple-element.33), channel_id=1, source_target_pairs={{0,1},{1,2},{2,3},{3,4},{4,5},{5,6},{6,7},{7,8},{8,9},{9,10},{10,1... | collective-permute-start | bytes 9224
  342.9 8.8 %collective-permute-start.16 = (f32[16,1152]{1,0:T(8,128)S(1)}, f32[16,1152]{1,0:T(8,128)S(1)}, u32[]{:S(2)}, u32[]{:S(2)}) collective-permute-start(f32[16,1152]{1,0:T(8,128)S(1)} %get-tuple-element.32), channel_id=1, source_target_pairs={{0,15},{1,16},{2,17},{3,18},{4,19},{5,20},{6,21},{7,22},{8,23},{9,... | collective-permute-start | bytes 221192
  344.2 10.4 %collective-permute-start.15 = (f32[16,1152]{1,0:T(8,128)S(1)}, f32[16,1152]{1,0:T(8,128)S(1)}, u32[]{:S(2)}, u32[]{:S(2)}) collective-permute-start(f32[16,1152]{1,0:T(8,128)S(1)} %get-tuple-element.32), channel_id=1, source_target_pairs={{0,14},{1,15},{2,16},{3,17},{4,18},{5,19},{6,20},{7,21},{8,22},{9,... | collective-permute-start | bytes 221192
  347.2 11.4 %collective-permute-start.14 = (f32[16,1152]{1,0:T(8,128)S(1)}, f32[16,1152]{1,0:T(8,128)S(1)}, u32[]{:S(2)}, u32[]{:S(2)}) collective-permute-start(f32[16,1152]{1,0:T(8,128)S(1)} %get-tuple-element.32), channel_id=1, source_target_pairs={{0,13},{1,14},{2,15},{3,16},{4,17},{5,18},{6,19},{7,20},{8,21},{9,... | collective-permute-start | bytes 221192
  348.8 11.7 %collective-permute-start.13 = (f32[16,1152]{1,0:T(8,128)S(1)}, f32[16,1152]{1,0:T(8,128)S(1)}, u32[]{:S(2)}, u32[]{:S(2)}) collective-permute-start(f32[16,1152]{1,0:T(8,128)S(1)} %get-tuple-element.32), channel_id=1, source_target_pairs={{0,12},{1,13},{2,14},{3,15},{4,16},{5,17},{6,18},{7,19},{8,20},{9,... | collective-permute-start | bytes 221192
  350.3 11.9 %collective-permute-start.12 = (f32[16,1152]{1,0:T(8,128)S(1)}, f32[16,1152]{1,0:T(8,128)S(1)}, u32[]{:S(2)}, u32[]{:S(2)}) collective-permute-start(f32[16,1152]{1,0:T(8,128)S(1)} %get-tuple-element.32), channel_id=1, source_target_pairs={{0,11},{1,12},{2,13},{3,14},{4,15},{5,16},{6,17},{7,18},{8,19},{9,... | collective-permute-start | bytes 221192
  351.6 155.7 %collective-permute-start.11 = (f32[16,1152]{1,0:T(8,128)S(1)}, f32[16,1152]{1,0:T(8,128)S(1)}, u32[]{:S(2)}, u32[]{:S(2)}) collective-permute-start(f32[16,1152]{1,0:T(8,128)S(1)} %get-tuple-element.32), channel_id=1, source_target_pairs={{0,10},{1,11},{2,12},{3,13},{4,14},{5,15},{6,16},{7,17},{8,18},{9,... | collective-permute-start | bytes 221192
  354.6 154.1 %collective-permute-start.10 = (f32[16,1152]{1,0:T(8,128)S(1)}, f32[16,1152]{1,0:T(8,128)S(1)}, u32[]{:S(2)}, u32[]{:S(2)}) collective-permute-start(f32[16,1152]{1,0:T(8,128)S(1)} %get-tuple-element.32), channel_id=1, source_target_pairs={{0,9},{1,10},{2,11},{3,12},{4,13},{5,14},{6,15},{7,16},{8,17},{9,1... | collective-permute-start | bytes 221192
  358.6 151.4 %collective-permute-start.9 = (f32[16,1152]{1,0:T(8,128)S(1)}, f32[16,1152]{1,0:T(8,128)S(1)}, u32[]{:S(2)}, u32[]{:S(2)}) collective-permute-start(f32[16,1152]{1,0:T(8,128)S(1)} %get-tuple-element.32), channel_id=1, source_target_pairs={{0,8},{1,9},{2,10},{3,11},{4,12},{5,13},{6,14},{7,15},{8,16},{9,17... | collective-permute-start | bytes 221192
  360.4 150.9 %collective-permute-start.8 = (f32[16,1152]{1,0:T(8,128)S(1)}, f32[16,1152]{1,0:T(8,128)S(1)}, u32[]{:S(2)}, u32[]{:S(2)}) collective-permute-start(f32[16,1152]{1,0:T(8,128)S(1)} %get-tuple-element.32), channel_id=1, source_target_pairs={{0,7},{1,8},{2,9},{3,10},{4,11},{5,12},{6,13},{7,14},{8,15},{9,16}... | collective-permute-start | bytes 221192
  362.3 150.3 %collective-permute-start.7 = (f32[16,1152]{1,0:T(8,128)S(1)}, f32[16,1152]{1,0:T(8,128)S(1)}, u32[]{:S(2)}, u32[]{:S(2)}) collective-permute-start(f32[16,1152]{1,0:T(8,128)S(1)} %get-tuple-element.32), channel_id=1, source_target_pairs={{0,6},{1,7},{2,8},{3,9},{4,10},{5,11},{6,12},{7,13},{8,14},{9,15},... | collective-permute-start | bytes 221192
  507.4 7.8 %collective-permute-start.6 = (f32[16,1152]{1,0:T(8,128)S(1)}, f32[16,1152]{1,0:T(8,128)S(1)}, u32[]{:S(2)}, u32[]{:S(2)}) collective-permute-start(f32[16,1152]{1,0:T(8,128)S(1)} %get-tuple-element.32), channel_id=1, source_target_pairs={{0,5},{1,6},{2,7},{3,8},{4,9},{5,10},{6,11},{7,12},{8,13},{9,14},{... | collective-permute-start | bytes 221192
  508.7 6.5 collective-permute-start.5
  (29 other events, 880.4 us)
Sparse Core Ops, SparseCore 0:
  94.0 547.0 all-reduce.8
where the time goes:
time: 662 us; the launch traced here: 650 us
  blocking collectives  310 us (47%)
  waiting for transfers between devices  123 us (19%)
  starting transfers between devices  86.3 us (13%)
  matrix products  72.8 us (11%)
  local copies, waits for them, and re-layouts  33.9 us (5%)
  between operations  16.6 us (3%)
  other arithmetic  8.24 us (1%)
    unnamed x2, blocking collectives  310 us
    unnamed x34, waiting for transfers between devices  122 us
    unnamed x33, starting transfers between devices  82.6 us
    unnamed x70, local copies, waits for them, and re-layouts  20.6 us
    sub x3, matrix products, attend(): weights = jnp.exp(scores - row_max)  16.8 us
  transfers between devices with their start and end apart: 35, of which 4 were waited for; matrix products, arithmetic and copies ran while one was open for 32% of the time, Pallas kernels for 0%

commit v1 on v0

--- a/solution.py
+++ b/solution.py
@@ -94,6 +94,13 @@
     )
 
 
+def sum_shares(share):
+    devices = lax.axis_size("tm")
+    pieces = share.astype(jnp.bfloat16).reshape(devices, share.shape[0] // devices, share.shape[1])
+    pieces = lax.all_to_all(pieces, "tm", split_axis=0, concat_axis=0, tiled=True)
+    return jnp.sum(pieces.astype(jnp.float32), axis=0)
+
+
 def local(strain, stem_weight, norm_gain, qkv_weight, out_weight, cotangent):
     features, inverse_rms, normed = embed_strain(strain, stem_weight, norm_gain)
     projected_rows = jnp.dot(normed, qkv_weight, preferred_element_type=jnp.float32).astype(
@@ -119,20 +126,11 @@
     grad_normed = grad_normed + contract_cols(returned, kv_weight)
     stem_term, gain_term = norm_back(grad_normed, features, inverse_rms, norm_gain, strain)
     result = contract_rows(normed, own_grads)
-    grad_qkv = lax.psum_scatter(
-        result.at[:, attention_span:].add(contract_rows(normed, returned)),
-        "tm",
-        scatter_dimension=0,
-        tiled=True,
-    )
-    grad_out = lax.psum_scatter(
-        contract_rows(cotangent, mixed), "tm", scatter_dimension=0, tiled=True
-    )
-    grad_stem, grad_gain = (
-        lax.psum_scatter(stem_term, "tm", scatter_dimension=0, tiled=True),
-        lax.psum_scatter(gain_term, "tm", scatter_dimension=0, tiled=True),
-    )
-    return (grad_qkv, grad_out, grad_stem, grad_gain)
+    result = result.at[:, attention_span:].add(contract_rows(normed, returned))
+    grad_out = sum_shares(contract_rows(cotangent, mixed))
+    packed = sum_shares(jnp.concatenate([result, stem_term, gain_term[:, None]], axis=1))
+    qkv_width = qkv_weight.shape[1]
+    return (packed[:, :qkv_width], grad_out, packed[:, qkv_width:-1], packed[:, -1])
 
 
 def solution(mesh):

time: 662 us -> 181 us (0.27); the launches traced: 650 us -> 180 us
  blocking collectives: 310 us -> 0 us
  waiting for transfers between devices: 123 us -> 49.6 us
  starting transfers between devices: 86.3 us -> 21.4 us
  between operations: 16.6 us -> 1.11 us
  matrix products: 72.8 us -> 64.3 us
  other arithmetic: 8.24 us -> 15.7 us
    unnamed x2 -> x0, blocking collectives: 310 us -> none
    unnamed x34 -> x0, waiting for transfers between devices: 122 us -> none
    unnamed x33 -> x0, starting transfers between devices: 82.6 us -> none
    all_to_all x0 -> x2, waiting for transfers between devices: none -> 32.8 us  [sum_shares(): lax.all_to_all(pieces, 'tm', split_axis=0, concat_axis=0, tiled=True)]
    all_to_all x0 -> x2, starting transfers between devices: none -> 17.8 us  [sum_shares(): lax.all_to_all(pieces, 'tm', split_axis=0, concat_axis=0, tiled=True)]
    unnamed x70 -> x50, local copies, waits for them, and re-layouts: 20.6 us -> 3.23 us
    ppermute x2, waiting for transfers between devices: 1.09 us -> 16.9 us  [passed_along(): lax.ppermute(shard, axis, [(i, (i + by) % devices) for i in range(devices)])]
    concatenate x0 -> x3, local copies, waits for them, and re-layouts: none -> 8.1 us  [local(): jnp.concatenate([result, stem_term, gain_term[:, None]], axis=1)]
  transfers between devices with their start and end apart: 35 -> 4, of which waited for: 4 -> 2; matrix products, arithmetic and copies ran while one was open for 32% -> 23% of each run, Pallas kernels for 0% -> 0%
where the time goes in v1:
time: 181 us; the launch traced here: 180 us
  matrix products  64.3 us (36%)
  waiting for transfers between devices  49.6 us (27%)
  local copies, waits for them, and re-layouts  28.2 us (16%)
  starting transfers between devices  21.4 us (12%)
  other arithmetic  15.7 us (9%)
    all_to_all x2, waiting for transfers between devices, sum_shares(): lax.all_to_all(pieces, 'tm', split_axis=0, concat_axis=0, tiled=True)  32.8 us
    all_to_all x2, starting transfers between devices, sum_shares(): lax.all_to_all(pieces, 'tm', split_axis=0, concat_axis=0, tiled=True)  17.8 us
    ppermute x2, waiting for transfers between devices, passed_along(): lax.ppermute(shard, axis, [(i, (i + by) % devices) for i in range(devices)])  16.9 us
    sub x3, matrix products, attend(): weights = jnp.exp(scores - row_max)  14.8 us
    dot_general x3, matrix products, attend(): jnp.einsum('jts,sd->tjd', probs_low, value_head, preferred_element_type=j...  11.2 us
    dot_general x3, matrix products, attend(): jnp.einsum('jts,tjd->sd', probs_low, grad_heads, preferred_element_type=j...  8.36 us
    concatenate x3, local copies, waits for them, and re-layouts, local(): jnp.concatenate([result, stem_term, gain_term[:, None]], axis=1)  8.1 us
    convert_element_type x3, other arithmetic, attend(): grad_scores = (probs * (grad_probs - delta)).astype(jnp.bfloat16)  7.38 us
  transfers between devices with their start and end apart: 4, of which 2 were waited for; matrix products, arithmetic and copies ran while one was open for 23% of the time, Pallas kernels for 0%

profile of v1, /device:TPU:1, one launch (start us, length us, event | category | flops | bytes accessed | tf_op | source)
XLA Modules:
  0.0 180.3 jit_solution(672803067627736415)
XLA Ops:
  1.9 1.5 fusion.42
  5.7 2.7 %collective-permute-start = (bf16[512,384]{1,0:T(8,128)(2,1)S(1)}, bf16[512,384]{1,0:T(8,128)(2,1)S(1)}, u32[]{:S(2)}, u32[]{:S(2)}) collective-permute-start(bf16[512,384]{1,0:T(8,128)(2,1)S(1)} %slice.170), channel_id=1, source_target_pairs={{0,1},{1,2},{2,3},{3,4},{4,5},{5,6},{6,7},{7,8},{8,9},{9,10},{10,1... | collective-permute-start | bytes 1179656 | tf_op jit(solution)/shard_map/ppermute | solution.py:15
  9.1 1.9 %convolution_convert_fusion.2 = bf16[512,768]{1,0:T(8,128)(2,1)S(1)} fusion(bf16[512,768]{1,0:T(8,128)(2,1)} %param.13, bf16[768,768]{1,0:T(8,128)(2,1)S(1)} %copy-done), kind=kOutput, calls=%fused_computation.72 | convolution fusion | flops 604372992 | bytes 2752512 | tf_op jit(solution)/shard_map/dot_general | solution.py:116
  15.2 5.1 %fusion.154 = (f32[4,512]{1,0:T(4,128)S(1)}, f32[4,512,1024]{1,2,0:T(8,128)}) fusion(bf16[512,4,64]{0,2,1:T(8,128)(2,1)S(1)} %bitcast.245, bf16[512,192]{1,0:T(8,128)(2,1)S(1)} %get-tuple-element.26, bf16[512,192]{1,0:T(8,128)(2,1)S(1)} %get-tuple-element.21), kind=kOutput, calls=%fused_computation.165 | convolution fusion | flops 274990080 | bytes 9052160 | tf_op jit(solution)/shard_map/sub | solution.py:58
  20.3 4.9 %fusion.90 = bf16[1024,64]{0,1:T(8,128)(2,1)S(1)} fusion(bf16[512,4,64]{0,2,1:T(8,128)(2,1)S(1)} %bitcast.252, f32[4,512,1024]{1,2,0:T(8,128)} %get-tuple-element.43, f32[4,512]{1,0:T(4,128)S(1)} %get-tuple-element.42), kind=kOutput, calls=%fused_computation.99 | convolution fusion | flops 272695296 | bytes 8790016 | tf_op jit(solution)/shard_map/jts,tjd->sd/dot_general | solution.py:73
  26.1 1.6 fusion.54
  29.0 2.4 %fusion.15 = bf16[4,512,1024]{1,2,0:T(8,128)(2,1)S(1)} fusion(f32[1024,512,4]{1,0,2:T(8,128)S(1)} %get-tuple-element.45, f32[4,512]{1,0:T(4,128)S(1)} %get-tuple-element.44, f32[4,512,1024]{1,2,0:T(8,128)S(1)} %copy-done.6, f32[4,512]{1,0:T(4,128)S(1)} %get-tuple-element.42), kind=kLoop, calls=%fused_computation.25 | loop fusion | flops 8388608 | bytes 20987904 | tf_op jit(solution)/shard_map/convert_element_type | solution.py:66
  33.6 4.9 %fusion.159 = (f32[4,512]{1,0:T(4,128)S(1)}, f32[4,512,1024]{1,2,0:T(8,128)}) fusion(bf16[512,4,64]{0,2,1:T(8,128)(2,1)S(1)} %bitcast.241, bf16[512,192]{1,0:T(8,128)(2,1)S(1)} %get-tuple-element.26, bf16[512,192]{1,0:T(8,128)(2,1)S(1)} %get-tuple-element.21), kind=kOutput, calls=%fused_computation.166 | convolution fusion | flops 274990080 | bytes 9052160 | tf_op jit(solution)/shard_map/sub | solution.py:58
  38.5 5.2 %fusion.57 = bf16[64,4,512]{2,0,1:T(8,128)(2,1)} fusion(bf16[512,192]{1,0:T(8,128)(2,1)S(1)} %get-tuple-element.27, bf16[512,192]{1,0:T(8,128)(2,1)S(1)} %copy-done.14, f32[4,512,1024]{1,2,0:T(8,128)} %get-tuple-element.47, f32[4,512]{1,0:T(4,128)S(1)} %get-tuple-element.46), kind=kOutput, calls=%fused_computation.79 | convolution fusion | flops 273022976 | bytes 9052160 | tf_op jit(solution)/shard_map/jts,sd->tjd/dot_general | solution.py:61
  47.1 2.6 %fusion.10 = bf16[4,512,1024]{1,2,0:T(8,128)(2,1)S(1)} fusion(f32[1024,512,4]{1,0,2:T(8,128)S(1)} %get-tuple-element.49, f32[4,512]{1,0:T(4,128)S(1)} %get-tuple-element.48, f32[4,512,1024]{1,2,0:T(8,128)S(1)} %copy-done.8, f32[4,512]{1,0:T(4,128)S(1)} %get-tuple-element.46), kind=kLoop, calls=%fused_computation.16 | loop fusion | flops 8388608 | bytes 20987904 | tf_op jit(solution)/shard_map/convert_element_type | solution.py:66
  52.1 4.8 %fusion.164 = (f32[4,512]{1,0:T(4,128)S(1)}, f32[4,512,1024]{1,2,0:T(8,128)}) fusion(bf16[512,4,64]{0,2,1:T(8,128)(2,1)S(1)} %bitcast.239, bf16[512,192]{1,0:T(8,128)(2,1)S(1)} %get-tuple-element.21, bf16[512,192]{1,0:T(8,128)(2,1)S(1)} %get-tuple-element.26), kind=kOutput, calls=%fused_computation.167 | convolution fusion | flops 274990080 | bytes 9052160 | tf_op jit(solution)/shard_map/sub | solution.py:58
  56.8 4.4 %fusion.60 = bf16[64,4,512]{2,0,1:T(8,128)(2,1)S(1)} fusion(bf16[512,192]{1,0:T(8,128)(2,1)S(1)} %copy-done.14, bf16[512,192]{1,0:T(8,128)(2,1)S(1)} %get-tuple-element.27, f32[4,512,1024]{1,2,0:T(8,128)} %get-tuple-element.51, f32[4,512]{1,0:T(4,128)S(1)} %get-tuple-element.50), kind=kOutput, calls=%fused_computation.80 | convolution fusion | flops 273022976 | bytes 9052160 | tf_op jit(solution)/shard_map/jts,sd->tjd/dot_general | solution.py:61
  62.6 2.1 %fusion.84 = bf16[1024,64]{0,1:T(8,128)(2,1)} fusion(bf16[512,4,64]{0,2,1:T(8,128)(2,1)S(1)} %bitcast.248, f32[4,512,1024]{1,2,0:T(8,128)S(1)} %copy-done.7, f32[4,512]{1,0:T(4,128)S(1)} %get-tuple-element.50), kind=kOutput, calls=%fused_computation.97 | convolution fusion | flops 272695296 | bytes 8790016 | tf_op jit(solution)/shard_map/jts,tjd->sd/dot_general | solution.py:73
  65.9 2.4 %fusion.5 = bf16[4,512,1024]{1,2,0:T(8,128)(2,1)S(1)} fusion(f32[1024,512,4]{1,0,2:T(8,128)S(1)} %get-tuple-element.53, f32[4,512]{1,0:T(4,128)S(1)} %get-tuple-element.52, f32[4,512,1024]{1,2,0:T(8,128)S(1)} %copy-done.7, f32[4,512]{1,0:T(4,128)S(1)} %get-tuple-element.50), kind=kLoop, calls=%fused_computation.7 | loop fusion | flops 8388608 | bytes 20987904 | tf_op jit(solution)/shard_map/convert_element_type | solution.py:66
  72.8 9.8 %all-to-all-start.1 = ((bf16[64,12,768]{2,1,0:T(8,128)(2,1)}), bf16[64,12,768]{2,1,0:T(8,128)(2,1)}, u32[]{:S(2)}, u32[]{:S(2)}) async-start(bf16[64,12,768]{2,1,0:T(8,128)(2,1)} %reshape.127), calls=%async_computation.1 | async-start | bytes 3145728 | tf_op jit(solution)/shard_map/all_to_all | solution.py:100
  83.8 2.8 %fusion.170 = f32[512,768]{1,0:T(8,128)S(1)} fusion(bf16[512,1152]{0,1:T(8,128)(2,1)S(1)} %get-tuple-element.29, bf16[768,1152]{1,0:T(8,128)(2,1)} %param.11), kind=kOutput, calls=%fused_computation.169 | convolution fusion | flops 905969664 | bytes 4521984 | tf_op jit(solution)/shard_map/dot_general | solution.py:92
  86.6 2.6 %fusion.169 = f32[768,1152]{1,0:T(8,128)S(1)} fusion(bf16[512,768]{1,0:T(8,128)(2,1)S(1)} %copy-done.5, bf16[512,1152]{0,1:T(8,128)(2,1)} %copy-done.9), kind=kOutput, calls=%fused_computation.168 | convolution fusion | flops 905969664 | bytes 5505024 | tf_op jit(solution)/shard_map/dot_general | solution.py:86
  89.2 16.9 %collective-permute-done.1 = bf16[512,384]{0,1:T(8,128)(2,1)S(1)} collective-permute-done((bf16[512,384]{0,1:T(8,128)(2,1)S(1)}, bf16[512,384]{0,1:T(8,128)(2,1)S(1)}, u32[]{:S(2)}, u32[]{:S(2)}) %collective-permute-start.1) | collective-permute-done | bytes 393248 | tf_op jit(solution)/shard_map/ppermute | solution.py:15
  106.1 2.1 %fusion.49 = (bf16[768]{0:T(1024)(128)(2,1)S(1)}, f32[512]{0:T(512)S(1)}, f32[512,768]{1,0:T(8,128)S(1)}) fusion(f32[512,768,1]{1,0,2:T(8,128)S(1)} %copy-done.3, f32[512]{0:T(512)S(1)} %add_rsqrt_fusion, f32[768]{0:T(1024)S(1)} %copy-done.17, f32[512,768]{1,0:T(8,128)S(1)} %fusion.170, bf16[512,384]{0,1:T(8,128)(2,1)S(1)} %collective-permute-done.1, ...), kind=kOutput, calls=%fused_computation.66 | convolution fusion | flops 304741120 | bytes 5710336 | tf_op jit(solution)/shard_map/dot_general | solution.py:92
  108.2 1.5 fusion.47
  109.7 3.0 %copy.110 = f32[768,512]{1,0:T(8,128)} copy(f32[768,512]{0,1:T(8,128)} %fusion.47) | data formatting | bytes 3145728 | tf_op jit(solution)/shard_map/sub | solution.py:31
  113.7 2.6 %dot_general.109 = f32[64,12,512]{2,1,0:T(8,128)} reshape(f32[768,512]{1,0:T(8,128)} %copy.110) | data formatting | bytes 3145728 | tf_op jit(solution)/shard_map/td,cts->dcs/dot_general | solution.py:34
  116.3 4.3 %fusion.78 = bf16[64,12,48]{0,2,1:T(8,128)(2,1)} fusion(bf16[48,512,1]{1,0,2:T(8,128)(2,1)} %bitcast.254, f32[64,12,512]{2,1,0:T(8,128)} %dot_general.109), kind=kOutput, calls=%fused_computation.93 | convolution fusion | flops 226529280 | bytes 1695744 | tf_op jit(solution)/shard_map/td,cts->dcs/dot_general | solution.py:34
  120.6 1.9 %copy.113 = bf16[64,12,48]{2,1,0:T(8,128)(2,1)} copy(bf16[64,12,48]{0,2,1:T(8,128)(2,1)} %fusion.78) | data formatting | bytes 147456 | tf_op jit(solution)/shard_map/convert.1
  122.4 2.0 %fusion.53 = f32[768,1152]{1,0:T(8,128)S(1)} fusion(f32[768,1152]{1,0:T(8,128)S(1)} %fusion.169, bf16[512,768]{1,0:T(8,128)(2,1)} %copy-done.4, bf16[512,384]{0,1:T(8,128)(2,1)} %copy-done.10), kind=kOutput, calls=%fused_computation.74 | convolution fusion | flops 302284800 | bytes 3538944 | tf_op jit(solution)/shard_map/dot_general | solution.py:86
  124.5 1.4 convert.41
  125.9 2.4 %concatenate.30 = bf16[64,12,1152]{2,1,0:T(8,128)(2,1)S(1)} reshape(bf16[768,1152]{1,0:T(8,128)(2,1)} %convert.41) | data formatting | bytes 3538944 | tf_op jit(solution)/shard_map/concatenate | solution.py:131
  128.3 4.7 %concatenate.32 = bf16[64,12,1201]{2,1,0:T(8,128)(2,1)} concatenate(bf16[64,12,1152]{2,1,0:T(8,128)(2,1)S(1)} %concatenate.30, bf16[64,12,48]{2,1,0:T(8,128)(2,1)} %copy.113, bf16[64,12,1]{2,1,0:T(8,128)(2,1)} %concatenate.34), dimensions={2} | concatenate | bytes 3689472 | tf_op jit(solution)/shard_map/concatenate | solution.py:131
  133.0 8.1 %all-to-all-start = ((bf16[64,12,1201]{2,1,0:T(8,128)(2,1)}), bf16[64,12,1201]{2,1,0:T(8,128)(2,1)}, u32[]{:S(2)}, u32[]{:S(2)}) async-start(bf16[64,12,1201]{2,1,0:T(8,128)(2,1)} %concatenate.32), calls=%async_computation | async-start | bytes 5242880 | tf_op jit(solution)/shard_map/all_to_all | solution.py:100
  141.1 2.3 %convert_reduce_fusion.1 = f32[12,768]{1,0:T(8,128)} fusion(bf16[64,12,768]{2,1,0:T(8,128)(2,1)} %all-to-all-done.1), kind=kLoop, calls=%fused_computation.40 | loop fusion | flops 1170432 | bytes 1216512 | tf_op jit(solution)/shard_map/reduce_sum | solution.py:101
  143.4 32.8 %all-to-all-done = bf16[64,12,1201]{2,1,0:T(8,128)(2,1)} async-done(((bf16[64,12,1201]{2,1,0:T(8,128)(2,1)}), bf16[64,12,1201]{2,1,0:T(8,128)(2,1)}, u32[]{:S(2)}, u32[]{:S(2)}) %all-to-all-start) | async-done | bytes 1844768 | tf_op jit(solution)/shard_map/all_to_all | solution.py:100
  176.2 2.2 %convert_reduce_fusion = f32[12,1201]{1,0:T(8,128)S(1)} fusion(bf16[64,12,1201]{2,1,0:T(8,128)(2,1)} %all-to-all-done), kind=kLoop, calls=%fused_computation.33 | loop fusion | flops 1830324 | bytes 1902384 | tf_op jit(solution)/shard_map/reduce_sum | solution.py:101
  (87 shorter events, 29.5 us)
Async XLA Ops:
  0.6 8.5 %copy-start = (bf16[768,768]{1,0:T(8,128)(2,1)S(1)}, bf16[768,768]{1,0:T(8,128)(2,1)}, u32[]{:S(2)}) copy-start(bf16[768,768]{1,0:T(8,128)(2,1)} %param.12) | copy-start | bytes 3538948
  1.9 2.5 %copy-start.15 = (bf16[768,1152]{1,0:T(8,128)(2,1)S(1)}, bf16[768,1152]{1,0:T(8,128)(2,1)}, u32[]{:S(2)}) copy-start(bf16[768,1152]{1,0:T(8,128)(2,1)} %param.11) | copy-start | bytes 5308420
  3.4 2.2 %copy-start.2 = (f32[512,768,1]{1,0,2:T(8,128)}, f32[512,768,1]{1,0,2:T(8,128)S(1)}, u32[]{:S(2)}) copy-start(f32[512,768,1]{1,0,2:T(8,128)S(1)} %get-tuple-element.41) | copy-start | bytes 4718596
  4.4 1.3 copy-start.4
  5.7 9.3 %collective-permute-start = (bf16[512,384]{1,0:T(8,128)(2,1)S(1)}, bf16[512,384]{1,0:T(8,128)(2,1)S(1)}, u32[]{:S(2)}, u32[]{:S(2)}) collective-permute-start(bf16[512,384]{1,0:T(8,128)(2,1)S(1)} %slice.170), channel_id=1, source_target_pairs={{0,1},{1,2},{2,3},{3,4},{4,5},{5,6},{6,7},{7,8},{8,9},{9,10},{10,1... | collective-permute-start | bytes 1179656 | tf_op jit(solution)/shard_map/ppermute | solution.py:15
  15.2 5.1 %copy-start.13 = (bf16[512,256]{0,1:T(8,128)(2,1)S(1)}, bf16[512,256]{0,1:T(8,128)(2,1)}, u32[]{:S(2)}) copy-start(bf16[512,256]{0,1:T(8,128)(2,1)} %copy.88) | copy-start | bytes 786436
  20.3 5.8 %copy-start.6 = (f32[4,512,1024]{1,2,0:T(8,128)S(1)}, f32[4,512,1024]{1,2,0:T(8,128)}, u32[]{:S(2)}) copy-start(f32[4,512,1024]{1,2,0:T(8,128)} %get-tuple-element.43) | copy-start | bytes 25165828
  20.3 5.8 %copy-start.14 = (bf16[512,192]{1,0:T(8,128)(2,1)S(1)}, bf16[512,192]{1,0:T(8,128)(2,1)}, u32[]{:S(2)}) copy-start(bf16[512,192]{1,0:T(8,128)(2,1)} %get-tuple-element.22) | copy-start | bytes 589828
  38.5 5.9 %copy-start.8 = (f32[4,512,1024]{1,2,0:T(8,128)S(1)}, f32[4,512,1024]{1,2,0:T(8,128)}, u32[]{:S(2)}) copy-start(f32[4,512,1024]{1,2,0:T(8,128)} %get-tuple-element.47) | copy-start | bytes 25165828
  38.5 5.9 %copy-start.12 = (bf16[512,256]{0,1:T(8,128)(2,1)S(1)}, bf16[512,256]{0,1:T(8,128)(2,1)}, u32[]{:S(2)}) copy-start(bf16[512,256]{0,1:T(8,128)(2,1)} %copy.94) | copy-start | bytes 786436
  56.8 5.8 %copy-start.7 = (f32[4,512,1024]{1,2,0:T(8,128)S(1)}, f32[4,512,1024]{1,2,0:T(8,128)}, u32[]{:S(2)}) copy-start(f32[4,512,1024]{1,2,0:T(8,128)} %get-tuple-element.51) | copy-start | bytes 25165828
  56.8 5.8 %copy-start.11 = (bf16[512,256]{0,1:T(8,128)(2,1)S(1)}, bf16[512,256]{0,1:T(8,128)(2,1)}, u32[]{:S(2)}) copy-start(bf16[512,256]{0,1:T(8,128)(2,1)} %copy.100) | copy-start | bytes 786436
  69.2 1.4 copy-start.18
  69.2 1.4 copy-start.19
  69.2 1.4 copy-start.20
  72.8 9.9 %copy-start.16 = (bf16[1024,64]{0,1:T(8,128)(2,1)S(1)}, bf16[1024,64]{0,1:T(8,128)(2,1)}, u32[]{:S(2)}) copy-start(bf16[1024,64]{0,1:T(8,128)(2,1)} %fusion.84) | copy-start | bytes 393220
  72.8 60.2 %all-to-all-start.1 = ((bf16[64,12,768]{2,1,0:T(8,128)(2,1)}), bf16[64,12,768]{2,1,0:T(8,128)(2,1)}, u32[]{:S(2)}, u32[]{:S(2)}) async-start(bf16[64,12,768]{2,1,0:T(8,128)(2,1)} %reshape.127), calls=%async_computation.1 | async-start | bytes 3145728 | tf_op jit(solution)/shard_map/all_to_all | solution.py:100
  82.8 1.0 copy-start.9
  82.8 23.3 %collective-permute-start.1 = (bf16[512,384]{0,1:T(8,128)(2,1)S(1)}, bf16[512,384]{0,1:T(8,128)(2,1)S(1)}, u32[]{:S(2)}, u32[]{:S(2)}) collective-permute-start(bf16[512,384]{0,1:T(8,128)(2,1)S(1)} %get-tuple-element.28), channel_id=1, source_target_pairs={{0,63},{1,0},{2,1},{3,2},{4,3},{5,4},{6,5},{7,6},{8,7},{9,8},{10,9... | collective-permute-start | bytes 1179656 | tf_op jit(solution)/shard_map/ppermute | solution.py:15
  83.8 2.8 %copy-start.5 = (bf16[512,768]{1,0:T(8,128)(2,1)S(1)}, bf16[512,768]{1,0:T(8,128)(2,1)}, u32[]{:S(2)}) copy-start(bf16[512,768]{1,0:T(8,128)(2,1)} %copy-done.4) | copy-start | bytes 2359300
  86.6 19.5 %copy-start.3 = (f32[512,768,1]{1,0,2:T(8,128)S(1)}, f32[512,768,1]{1,0,2:T(8,128)}, u32[]{:S(2)}) copy-start(f32[512,768,1]{1,0,2:T(8,128)} %copy-done.2) | copy-start | bytes 4718596
  86.6 19.5 %copy-start.17 = (f32[768]{0:T(1024)S(1)}, f32[768]{0:T(1024)}, u32[]{:S(2)}) copy-start(f32[768]{0:T(1024)} %param.10) | copy-start | bytes 9220
  106.1 2.1 %copy-start.10 = (bf16[512,384]{0,1:T(8,128)(2,1)}, bf16[512,384]{0,1:T(8,128)(2,1)S(1)}, u32[]{:S(2)}) copy-start(bf16[512,384]{0,1:T(8,128)(2,1)S(1)} %collective-permute-done.1) | copy-start | bytes 1179652
  128.3 52.0 %copy-start.1 = (bf16[768,768]{1,0:T(8,128)(2,1)S(1)}, bf16[768,768]{1,0:T(8,128)(2,1)}, u32[]{:S(2)}) copy-start(bf16[768,768]{1,0:T(8,128)(2,1)} %param.12) | copy-start | bytes 3538948
  133.0 43.2 %all-to-all-start = ((bf16[64,12,1201]{2,1,0:T(8,128)(2,1)}), bf16[64,12,1201]{2,1,0:T(8,128)(2,1)}, u32[]{:S(2)}, u32[]{:S(2)}) async-start(bf16[64,12,1201]{2,1,0:T(8,128)(2,1)} %concatenate.32), calls=%async_computation | async-start | bytes 5242880 | tf_op jit(solution)/shard_map/all_to_all | solution.py:100

commit v2 on v1

v2 whole, which is shorter than its diff:
```python
import functools
import math

import jax
import jax.numpy as jnp
from jax import lax
from jax.experimental import pallas as pl
from jax.experimental.pallas import tpu as pltpu
from jax.sharding import PartitionSpec as P

HEAD_SIZE = 64
STRIDE = 16
GROUP_HEADS = 4
GROUPS = 3

EPSILON = 1e-05
BF16 = jnp.bfloat16
F32 = jnp.float32
HEAD_SCALE = HEAD_SIZE ** (-0.5)
EXP_SCALE = HEAD_SCALE * math.log2(math.e)
VMEM_LIMIT = 32 * 2**20


def passed_along(shard, axis, by):
    devices = lax.axis_size(axis)
    return lax.ppermute(shard, axis, [(i, (i + by) % devices) for i in range(devices)])


def nn(left, right):
    return lax.dot_general(left, right, (((1,), (0,)), ((), ())), preferred_element_type=F32)


def nt(left, right):
    return lax.dot_general(left, right, (((1,), (1,)), ((), ())), preferred_element_type=F32)


def attend_kernel(
    group, q_ref, g_ref, prev_ref, own_ref, cot_ref, normed_ref,
    share_ref, dq_ref, prev_grad_ref, own_grad_ref, mixed_ref,
):
    half = own_ref.shape[1] // 2
    rows = own_ref.shape[0]
    key_cols = slice(group * HEAD_SIZE, (group + 1) * HEAD_SIZE)
    value_cols = slice(half + group * HEAD_SIZE, half + (group + 1) * HEAD_SIZE)
    keys = jnp.concatenate([prev_ref[:, key_cols], own_ref[:, key_cols]], axis=0)
    values = jnp.concatenate([prev_ref[:, value_cols], own_ref[:, value_cols]], axis=0)
    keys_t = keys.T
    values_t = jnp.concatenate([values.T, jnp.ones((16, values.shape[0]), BF16)], axis=0)
    grad_keys = None
    grad_values = None
    for head in range(GROUP_HEADS):
        head_rows = slice(head * HEAD_SIZE, (head + 1) * HEAD_SIZE)
        query = q_ref[head_rows, :]
        grad = g_ref[head_rows, :]
        scores = nn(keys, query)
        top = jnp.max(scores, axis=0, keepdims=True)
        weights = jnp.exp2(scores * EXP_SCALE - top * EXP_SCALE)
        weights_low = weights.astype(BF16)
        mixed = nn(values_t, weights_low)
        inverse = 1.0 / mixed[HEAD_SIZE : HEAD_SIZE + 1]
        mixed = mixed[:HEAD_SIZE] * inverse
        mixed_ref[head_rows, :] = mixed.astype(BF16)
        grad_wide = grad.astype(F32)
        delta = jnp.sum(mixed * grad_wide, axis=0, keepdims=True)
        grad_scores = (weights * (nn(values, grad) - delta)).astype(BF16)
        scaled = inverse * HEAD_SCALE
        dq_ref[head_rows, :] = (nn(keys_t, grad_scores) * scaled).astype(BF16)
        key_part = nt(grad_scores, (query.astype(F32) * scaled).astype(BF16))
        value_part = nt(weights_low, (grad_wide * inverse).astype(BF16))
        grad_keys = key_part if grad_keys is None else grad_keys + key_part
        grad_values = value_part if grad_values is None else grad_values + value_part
    both = jnp.concatenate([grad_keys, grad_values], axis=1).astype(BF16)
    prev_grad_ref[...] = both[:rows]
    own_grad_ref[...] = both[rows:]
    width = mixed_ref.shape[0]
    share_ref[:, :width] = nt(cot_ref[...], mixed_ref[...]).astype(BF16)
    share_ref[:, width:] = nt(normed_ref[...], dq_ref[...]).astype(BF16)


def whole(array):
    return pl.BlockSpec(array.shape, lambda step: (0,) * array.ndim)


def attend_group(group, q_t, g_t, prev_pairs, own_pairs, cot_t, normed_t):
    tokens = own_pairs.shape[0]
    width = GROUP_HEADS * HEAD_SIZE
    outs = [
        jax.ShapeDtypeStruct((cot_t.shape[0], 2 * width), BF16),
        jax.ShapeDtypeStruct((width, tokens), BF16),
        jax.ShapeDtypeStruct((tokens, 2 * HEAD_SIZE), BF16),
        jax.ShapeDtypeStruct((tokens, 2 * HEAD_SIZE), BF16),
    ]
    block = pl.BlockSpec((width, tokens), lambda step: (group, 0))
    return pl.pallas_call(
        functools.partial(attend_kernel, group),
        grid=(1,),
        in_specs=[block, block] + [whole(a) for a in (prev_pairs, own_pairs, cot_t, normed_t)],
        out_specs=[whole(a) for a in outs],
        out_shape=outs,
        scratch_shapes=[pltpu.VMEM((width, tokens), BF16)],
        compiler_params=pltpu.CompilerParams(vmem_limit_bytes=VMEM_LIMIT),
        cost_estimate=pl.CostEstimate(
            flops=2 * 7 * 4 * 512 * 1024 * 64, bytes_accessed=5 * 2**20, transcendentals=2**21
        ),
        name=f"attend_{group}",
    )(q_t, g_t, prev_pairs, own_pairs, cot_t, normed_t)


def tail_kernel(
    dq0, dq1, dq2, own0, own1, own2, back0, back1, back2,
    weight_ref, patches_ref, stem_ref, gain_ref, normed_ref, out_ref,
):
    def joined(parts):
        parts = [part[...] for part in parts]
        return jnp.concatenate(
            [part[:, :HEAD_SIZE] for part in parts] + [part[:, HEAD_SIZE:] for part in parts], axis=1
        )

    own = joined((own0, own1, own2))
    back = joined((back0, back1, back2))
    dq = jnp.concatenate([dq0[...], dq1[...], dq2[...]], axis=0)
    span = dq.shape[0]
    patches = patches_ref[...]
    features = nt(stem_ref[...], patches)
    inverse_rms = lax.rsqrt(jnp.mean(features * features, axis=0, keepdims=True) + EPSILON)
    kv_weight = weight_ref[:, span:]
    grad_normed = nn(weight_ref[:, :span], dq) + nt(kv_weight, own) + nt(kv_weight, back)
    scaled = grad_normed * gain_ref[...]
    inner = jnp.mean(scaled * features, axis=0, keepdims=True)
    gain_term = jnp.sum(grad_normed * features * inverse_rms, axis=1, keepdims=True)
    grad_features = inverse_rms * scaled - features * (inverse_rms**3 * inner)
    high = grad_features.astype(BF16)
    low = (grad_features - high.astype(F32)).astype(BF16)
    stem_term = nn(high, patches) + nn(low, patches)
    normed = normed_ref[...]
    kv_term = nn(normed, own) + nn(normed, back)
    kv_width = kv_term.shape[1]
    out_ref[:, :kv_width] = kv_term.astype(BF16)
    spare = jnp.zeros((span, out_ref.shape[1] - kv_width - stem_term.shape[1] - 1), F32)
    out_ref[:, kv_width:] = jnp.concatenate([stem_term, gain_term, spare], axis=1).astype(BF16)


def tail(dqs, owns, backs, weight, patches, stem, gain, normed_t):
    out = jax.ShapeDtypeStruct((normed_t.shape[0], 512), BF16)
    args = (*dqs, *owns, *backs, weight, patches, stem, gain, normed_t)
    return pl.pallas_call(
        tail_kernel,
        grid=(1,),
        in_specs=[whole(a) for a in args],
        out_specs=whole(out),
        out_shape=out,
        compiler_params=pltpu.CompilerParams(vmem_limit_bytes=VMEM_LIMIT),
        name="tail",
    )(*args)


def spread_shares(share):
    devices = lax.axis_size("tm")
    pieces = share.reshape(devices, share.shape[0] // devices, share.shape[1])
    return lax.all_to_all(pieces, "tm", split_axis=0, concat_axis=0, tiled=True)


def summed(pieces):
    return jnp.sum(pieces.astype(F32), axis=0)


def local(strain, stem_weight, norm_gain, qkv_weight, out_weight, cotangent):
    channels = strain.shape[0]
    span = out_weight.shape[1]
    patches = strain.reshape(channels, -1, STRIDE).transpose(1, 0, 2).reshape(-1, channels * STRIDE)
    features = nt(patches, stem_weight)
    inverse_rms = lax.rsqrt(jnp.mean(features * features, axis=-1, keepdims=True) + EPSILON)
    normed = (features * inverse_rms * norm_gain).astype(BF16)
    own_pairs = nn(normed, qkv_weight[:, span:]).astype(BF16)
    prev_pairs = passed_along(own_pairs, "tm", 1)
    q_t = lax.dot_general(
        qkv_weight[:, :span], normed, (((0,), (1,)), ((), ())), preferred_element_type=F32
    ).astype(BF16)
    g_t = lax.dot_general(
        out_weight, cotangent, (((0,), (1,)), ((), ())), preferred_element_type=F32
    ).astype(BF16)
    cot_t = cotangent.T
    normed_t = normed.T
    dqs, owns, backs, sums = [], [], [], []
    for group in range(GROUPS):
        share, dq, prev_grad, own_grad = attend_group(
            group, q_t, g_t, prev_pairs, own_pairs, cot_t, normed_t
        )
        sums.append(spread_shares(share))
        dqs.append(dq)
        owns.append(own_grad)
        backs.append(passed_along(prev_grad, "tm", -1))
    packed = tail(
        dqs, owns, backs, qkv_weight, patches, stem_weight, norm_gain[:, None], normed_t
    )
    sums = [summed(s) for s in sums]
    last = summed(spread_shares(packed))
    width = GROUP_HEADS * HEAD_SIZE
    kv_width = qkv_weight.shape[1] - span
    patch = stem_weight.shape[1]
    grad_qkv = jnp.concatenate([s[:, width:] for s in sums] + [last[:, :kv_width]], axis=1)
    grad_out = jnp.concatenate([s[:, :width] for s in sums], axis=1)
    return (
        grad_qkv,
        grad_out,
        last[:, kv_width : kv_width + patch],
        last[:, kv_width + patch],
    )


def solution(mesh):
    in_specs = (P(None, ("sim", "tm")), P(), P(), P(), P(), P(("sim", "tm"), None))
    out_specs = (
        P(("sim", "tm"), None),
        P(("sim", "tm"), None),
        P(("sim", "tm"), None),
        P(("sim", "tm")),
    )
    return jax.shard_map(local, mesh=mesh, in_specs=in_specs, out_specs=out_specs, check_vma=False)
```

time: 181 us -> 153 us (0.85)
  matrix products: 64.3 us -> 8.13 us
  Pallas kernels: 0 us -> 28 us
  starting transfers between devices: 21.4 us -> 39 us
  waiting for transfers between devices: 49.6 us -> 32.2 us
  other arithmetic: 15.7 us -> 5.97 us
  local copies, waits for them, and re-layouts: 28.2 us -> 37.8 us
    dot_general x24 -> x4, matrix products: 49.5 us -> 8.13 us  [the longest x1 2.73 us: local(): lax.dot_general(qkv_weight[:, :span], normed, (((0,), (1,)), ((), ())), p...]
    pallas_call x0 -> x4, Pallas kernels: none -> 28 us  [the longest x3 24.6 us: attend_group(): pl.pallas_call(functools.partial(attend_kernel, group), grid=(1,), in_spe...]
    unnamed x50 -> x82, local copies, waits for them, and re-layouts: 3.23 us -> 28.5 us
    sub x3 -> x0, matrix products: 14.8 us -> none  [attend(): weights = jnp.exp(scores - row_max)]
    all_to_all x2 -> x4, starting transfers between devices: 17.8 us -> 29.6 us  [spread_shares(): return lax.all_to_all(pieces, 'tm', split_axis=0, concat_axis=0, tiled=True)]
    all_to_all x2 -> x4, waiting for transfers between devices: 32.8 us -> 22.8 us  [spread_shares(): return lax.all_to_all(pieces, 'tm', split_axis=0, concat_axis=0, tiled=True)]
    concatenate x4 -> x0, local copies, waits for them, and re-layouts: 8.11 us -> none  [the longest x3 8.1 us: local(): jnp.concatenate([result, stem_term, gain_term[:, None]], axis=1)]
    convert_element_type x4 -> x1, other arithmetic: 8.31 us -> 0.21 us  [local(): normed = (features * inverse_rms * norm_gain).astype(BF16)]
  transfers between devices with their start and end apart: 4 -> 8, of which waited for: 2 -> 6; matrix products, arithmetic and copies ran while one was open for 23% -> 10% of each run, Pallas kernels for 0% -> 13%
where the time goes in v2:
time: 153 us; the launch traced here: 152 us
  starting transfers between devices  39 us (25%)
  local copies, waits for them, and re-layouts  37.8 us (25%)
  waiting for transfers between devices  32.2 us (21%)
  Pallas kernels  28 us (18%)
  matrix products  8.13 us (5%)
  other arithmetic  5.97 us (4%)
    all_to_all x4, starting transfers between devices, spread_shares(): return lax.all_to_all(pieces, 'tm', split_axis=0, concat_axis=0, tiled=True)  29.6 us
    unnamed x82, local copies, waits for them, and re-layouts  28.5 us
    pallas_call x3, Pallas kernels, attend_group(): pl.pallas_call(functools.partial(attend_kernel, group), grid=(1,), in_spe...  24.6 us
    all_to_all x4, waiting for transfers between devices, spread_shares(): return lax.all_to_all(pieces, 'tm', split_axis=0, concat_axis=0, tiled=True)  22.8 us
    ppermute x4, starting transfers between devices, passed_along(): lax.ppermute(shard, axis, [(i, (i + by) % devices) for i in range(devices)])  9.4 us
    ppermute x4, waiting for transfers between devices, passed_along(): lax.ppermute(shard, axis, [(i, (i + by) % devices) for i in range(devices)])  9.33 us
    reshape x4, local copies, waits for them, and re-layouts, spread_shares(): pieces = share.reshape(devices, share.shape[0] // devices, share.shape[1])  4.66 us
    reduce_sum x4, other arithmetic, summed(): return jnp.sum(pieces.astype(F32), axis=0)  4.49 us
  transfers between devices with their start and end apart: 8, of which 6 were waited for; matrix products, arithmetic and copies ran while one was open for 10% of the time, Pallas kernels for 13%

profile of v2, /device:TPU:1, one launch (start us, length us, event | category | flops | bytes accessed | tf_op | source)
XLA Modules:
  0.0 151.9 jit_solution(15335775277173009182)
XLA Ops:
  0.6 1.2 reshape.35
  2.0 1.4 multiply_reduce_fusion
  3.4 1.7 %copy.16 = f32[512,768]{0,1:T(8,128)} copy(f32[512,768]{1,0:T(8,128)S(1)} %get-tuple-element.35) | data formatting | bytes 3145728 | tf_op jit(solution)/shard_map/dot_general | solution.py:34
  5.1 2.3 %convolution_convert_fusion.2.own_ref = bf16[512,384]{1,0:T(8,128)(2,1)S(1)} fusion(bf16[768,1152]{1,0:T(8,128)(2,1)} %weight_ref.1, f32[512,768]{0,1:T(8,128)} %copy.16, f32[768]{0:T(1024)S(1)} %copy-done.39, f32[512]{0:T(512)S(1)} %add_rsqrt_fusion), kind=kOutput, calls=%fused_computation.9 | convolution fusion | flops 303366144 | bytes 2561024 | tf_op jit(solution)/shard_map/dot_general | solution.py:30
  7.4 2.7 %collective-permute-start = (bf16[512,384]{1,0:T(8,128)(2,1)S(1)}, bf16[512,384]{1,0:T(8,128)(2,1)S(1)}, u32[]{:S(2)}, u32[]{:S(2)}) collective-permute-start(bf16[512,384]{1,0:T(8,128)(2,1)S(1)} %convolution_convert_fusion.2.own_ref), channel_id=1, source_target_pairs={{0,1},{1,2},{2,3},{3,4},{4,5},{5,6},{6,7},{7,8},{8,9},{9,10},{10,1... | collective-permute-start | bytes 1179656 | tf_op jit(solution)/shard_map/ppermute | solution.py:26
  10.1 1.7 %convolution_convert_fusion.g_ref = bf16[768,512]{1,0:T(8,128)(2,1)} fusion(bf16[768,768]{1,0:T(8,128)(2,1)S(1)} %copy-done, bf16[512,768]{1,0:T(8,128)(2,1)S(1)} %copy-done.35), kind=kOutput, calls=%fused_computation.6 | convolution fusion | flops 604372992 | bytes 2752512 | tf_op jit(solution)/shard_map/dot_general | solution.py:179
  12.1 1.4 copy.18
  13.5 2.7 %fusion.q_ref = bf16[768,512]{1,0:T(8,128)(2,1)S(1)} fusion(bf16[768,1152]{1,0:T(8,128)(2,1)} %weight_ref.1, f32[512,768]{0,1:T(8,128)} %copy.16, f32[768]{0:T(1024)S(1)} %copy-done.39, f32[512]{0:T(512)S(1)} %add_rsqrt_fusion), kind=kOutput, calls=%fused_computation.8 | convolution fusion | flops 605552640 | bytes 3544064 | tf_op jit(solution)/shard_map/dot_general | solution.py:176
  18.0 8.2 %attend_2.1 = (bf16[768,512]{1,0:T(8,128)(2,1)S(1)}, bf16[256,512]{1,0:T(8,128)(2,1)S(1)}, bf16[512,128]{1,0:T(8,128)(2,1)}, bf16[512,128]{1,0:T(8,128)(2,1)S(1)}) custom-call(bf16[768,512]{1,0:T(8,128)(2,1)S(1)} %fusion.q_ref, bf16[768,512]{1,0:T(8,128)(2,1)S(1)} %copy-done.31, bf16[512,384]{1,0:T(8,128)(2,1)S(1)} %copy-done.25, ...), custom_call_target="tpu_custom_call" | custom-call | flops 1879048192 | bytes 5242880 | tf_op jit(solution)/shard_map/attend_2/pallas_call | solution.py:94
  28.4 1.1 reshape.39
  29.6 10.0 %all-to-all-start.2 = ((bf16[64,12,512]{2,1,0:T(8,128)(2,1)}), bf16[64,12,512]{2,1,0:T(8,128)(2,1)}, u32[]{:S(2)}, u32[]{:S(2)}) async-start(bf16[64,12,512]{2,1,0:T(8,128)(2,1)} %reshape.39), calls=%async_computation.2 | async-start | bytes 2097152 | tf_op jit(solution)/shard_map/all_to_all | solution.py:160
  41.6 1.1 copy-done.29
  43.8 8.2 %attend_1.1 = (bf16[768,512]{1,0:T(8,128)(2,1)S(1)}, bf16[256,512]{1,0:T(8,128)(2,1)S(1)}, bf16[512,128]{1,0:T(8,128)(2,1)}, bf16[512,128]{1,0:T(8,128)(2,1)S(1)}) custom-call(bf16[768,512]{1,0:T(8,128)(2,1)S(1)} %copy-done.29, bf16[768,512]{1,0:T(8,128)(2,1)S(1)} %copy-done.32, bf16[512,384]{1,0:T(8,128)(2,1)S(1)} %copy-done.26, ...), custom_call_target="tpu_custom_call" | custom-call | flops 1879048192 | bytes 5242880 | tf_op jit(solution)/shard_map/attend_1/pallas_call | solution.py:94
  53.4 1.2 reshape.38
  54.6 3.3 %all-to-all-done.2 = bf16[64,12,512]{2,1,0:T(8,128)(2,1)} async-done(((bf16[64,12,512]{2,1,0:T(8,128)(2,1)}), bf16[64,12,512]{2,1,0:T(8,128)(2,1)}, u32[]{:S(2)}, u32[]{:S(2)}) %all-to-all-start.2) | async-done | bytes 786464 | tf_op jit(solution)/shard_map/all_to_all | solution.py:160
  57.9 5.8 %all-to-all-start.1 = ((bf16[64,12,512]{2,1,0:T(8,128)(2,1)}), bf16[64,12,512]{2,1,0:T(8,128)(2,1)}, u32[]{:S(2)}, u32[]{:S(2)}) async-start(bf16[64,12,512]{2,1,0:T(8,128)(2,1)} %reshape.38), calls=%async_computation.1 | async-start | bytes 2097152 | tf_op jit(solution)/shard_map/all_to_all | solution.py:160
  65.7 1.1 copy-done.30
  66.9 1.1 copy-done.33
  68.0 8.2 %attend_0.1 = (bf16[768,512]{1,0:T(8,128)(2,1)S(1)}, bf16[256,512]{1,0:T(8,128)(2,1)S(1)}, bf16[512,128]{1,0:T(8,128)(2,1)}, bf16[512,128]{1,0:T(8,128)(2,1)S(1)}) custom-call(bf16[768,512]{1,0:T(8,128)(2,1)S(1)} %copy-done.30, bf16[768,512]{1,0:T(8,128)(2,1)S(1)} %copy-done.33, bf16[512,384]{1,0:T(8,128)(2,1)S(1)} %copy-done.27, ...), custom_call_target="tpu_custom_call" | custom-call | flops 1879048192 | bytes 5242880 | tf_op jit(solution)/shard_map/attend_0/pallas_call | solution.py:94
  77.5 1.2 reshape.37
  78.7 3.3 %all-to-all-done.1 = bf16[64,12,512]{2,1,0:T(8,128)(2,1)} async-done(((bf16[64,12,512]{2,1,0:T(8,128)(2,1)}), bf16[64,12,512]{2,1,0:T(8,128)(2,1)}, u32[]{:S(2)}, u32[]{:S(2)}) %all-to-all-start.1) | async-done | bytes 786464 | tf_op jit(solution)/shard_map/all_to_all | solution.py:160
  82.0 5.9 %all-to-all-start = ((bf16[64,12,512]{2,1,0:T(8,128)(2,1)}), bf16[64,12,512]{2,1,0:T(8,128)(2,1)}, u32[]{:S(2)}, u32[]{:S(2)}) async-start(bf16[64,12,512]{2,1,0:T(8,128)(2,1)} %reshape.37), calls=%async_computation | async-start | bytes 2097152 | tf_op jit(solution)/shard_map/all_to_all | solution.py:160
  88.4 5.8 %collective-permute-start.2 = (bf16[512,128]{1,0:T(8,128)(2,1)}, bf16[512,128]{1,0:T(8,128)(2,1)S(1)}, u32[]{:S(2)}, u32[]{:S(2)}) collective-permute-start(bf16[512,128]{1,0:T(8,128)(2,1)} %get-tuple-element.26), channel_id=1, source_target_pairs={{0,63},{1,0},{2,1},{3,2},{4,3},{5,4},{6,5},{7,6},{8,7},{9,8},{10,9... | collective-permute-start | bytes 393224 | tf_op jit(solution)/shard_map/ppermute | solution.py:26
  95.1 7.8 %collective-permute-done.3.back2 = bf16[512,128]{1,0:T(8,128)(2,1)S(1)} collective-permute-done((bf16[512,128]{1,0:T(8,128)(2,1)}, bf16[512,128]{1,0:T(8,128)(2,1)S(1)}, u32[]{:S(2)}, u32[]{:S(2)}) %collective-permute-start.3) | collective-permute-done | bytes 131104 | tf_op jit(solution)/shard_map/ppermute | solution.py:26
  106.3 1.5 copy-done.1
  116.1 3.4 %tail.1 = bf16[768,512]{1,0:T(8,128)(2,1)S(1)} custom-call(bf16[256,512]{1,0:T(8,128)(2,1)S(1)} %copy-done.7, bf16[256,512]{1,0:T(8,128)(2,1)S(1)} %copy-done.5, bf16[256,512]{1,0:T(8,128)(2,1)S(1)} %copy-done.3, bf16[512,128]{1,0:T(8,128)(2,1)S(1)} %copy-done.13, bf16[512,128]{1,0:T(8,128)(2,1)S(1)} %copy-done.11, bf16[512,128]{1,0:T(8,128)(2,1)S(1)} %copy-done.9, ...), custom_call_target="tpu_custom_call" | custom-call | tf_op jit(solution)/shard_map/tail/pallas_call | solution.py:146
  119.5 1.2 reshape.40
  120.7 1.4 convert_reduce_fusion.1
  122.1 1.4 convert_reduce_fusion.2
  123.5 7.9 %all-to-all-start.3 = ((bf16[64,12,512]{2,1,0:T(8,128)(2,1)}), bf16[64,12,512]{2,1,0:T(8,128)(2,1)S(1)}, u32[]{:S(2)}, u32[]{:S(2)}) async-start(bf16[64,12,512]{2,1,0:T(8,128)(2,1)} %reshape.40), calls=%async_computation.3 | async-start | bytes 2097152 | tf_op jit(solution)/shard_map/all_to_all | solution.py:160
  131.4 1.4 convert_reduce_fusion.3
  133.5 16.2 %all-to-all-done.3 = bf16[64,12,512]{2,1,0:T(8,128)(2,1)S(1)} async-done(((bf16[64,12,512]{2,1,0:T(8,128)(2,1)}), bf16[64,12,512]{2,1,0:T(8,128)(2,1)S(1)}, u32[]{:S(2)}, u32[]{:S(2)}) %all-to-all-start.3) | async-done | bytes 786464 | tf_op jit(solution)/shard_map/all_to_all | solution.py:160
  (97 shorter events, 28.1 us)
Async XLA Ops:
  0.6 9.5 %copy-start = (bf16[768,768]{1,0:T(8,128)(2,1)S(1)}, bf16[768,768]{1,0:T(8,128)(2,1)}, u32[]{:S(2)}) copy-start(bf16[768,768]{1,0:T(8,128)(2,1)} %param.10) | copy-start | bytes 3538948
  2.0 3.0 %copy-start.36 = (bf16[512,3,16]{0,2,1:T(8,128)(2,1)}, bf16[512,3,16]{0,2,1:T(8,128)(2,1)S(1)}, u32[]{:S(2)}) copy-start(bf16[512,3,16]{0,2,1:T(8,128)(2,1)S(1)} %copy.15) | copy-start | bytes 147460
  3.4 1.7 %copy-start.39 = (f32[768]{0:T(1024)S(1)}, f32[768]{0:T(1024)}, u32[]{:S(2)}) copy-start(f32[768]{0:T(1024)} %param.8) | copy-start | bytes 9220
  5.1 5.0 %copy-start.35 = (bf16[512,768]{1,0:T(8,128)(2,1)S(1)}, bf16[512,768]{1,0:T(8,128)(2,1)}, u32[]{:S(2)}) copy-start(bf16[512,768]{1,0:T(8,128)(2,1)} %param.11) | copy-start | bytes 2359300
  7.4 4.4 %copy-start.20 = (bf16[512,384]{1,0:T(8,128)(2,1)}, bf16[512,384]{1,0:T(8,128)(2,1)S(1)}, u32[]{:S(2)}) copy-start(bf16[512,384]{1,0:T(8,128)(2,1)S(1)} %convolution_convert_fusion.2.own_ref) | copy-start | bytes 1179652
  7.4 4.4 %copy-start.34 = (f32[512,768]{0,1:T(8,128)S(1)}, f32[512,768]{0,1:T(8,128)}, u32[]{:S(2)}) copy-start(f32[512,768]{0,1:T(8,128)} %copy.16) | copy-start | bytes 4718596
  7.4 8.8 %collective-permute-start = (bf16[512,384]{1,0:T(8,128)(2,1)S(1)}, bf16[512,384]{1,0:T(8,128)(2,1)S(1)}, u32[]{:S(2)}, u32[]{:S(2)}) collective-permute-start(bf16[512,384]{1,0:T(8,128)(2,1)S(1)} %convolution_convert_fusion.2.own_ref), channel_id=1, source_target_pairs={{0,1},{1,2},{2,3},{3,4},{4,5},{5,6},{6,7},{7,8},{8,9},{9,10},{10,1... | collective-permute-start | bytes 1179656 | tf_op jit(solution)/shard_map/ppermute | solution.py:26
  13.5 3.5 %copy-start.21 = (bf16[512,384]{1,0:T(8,128)(2,1)S(1)}, bf16[512,384]{1,0:T(8,128)(2,1)}, u32[]{:S(2)}) copy-start(bf16[512,384]{1,0:T(8,128)(2,1)} %copy-done.20) | copy-start | bytes 1179652
  13.5 3.5 %copy-start.31 = (bf16[768,512]{1,0:T(8,128)(2,1)S(1)}, bf16[768,512]{1,0:T(8,128)(2,1)}, u32[]{:S(2)}) copy-start(bf16[768,512]{1,0:T(8,128)(2,1)} %convolution_convert_fusion.g_ref) | copy-start | bytes 2359300
  17.0 1.0 copy-start.25
  27.5 0.9 copy-start.28
  29.6 28.3 %all-to-all-start.2 = ((bf16[64,12,512]{2,1,0:T(8,128)(2,1)}), bf16[64,12,512]{2,1,0:T(8,128)(2,1)}, u32[]{:S(2)}, u32[]{:S(2)}) async-start(bf16[64,12,512]{2,1,0:T(8,128)(2,1)} %reshape.39), calls=%async_computation.2 | async-start | bytes 2097152 | tf_op jit(solution)/shard_map/all_to_all | solution.py:160
  39.6 1.0 copy-start.22
  40.6 1.0 copy-start.26
  41.6 1.1 copy-start.29
  42.7 1.1 copy-start.32
  57.9 24.1 %all-to-all-start.1 = ((bf16[64,12,512]{2,1,0:T(8,128)(2,1)}), bf16[64,12,512]{2,1,0:T(8,128)(2,1)}, u32[]{:S(2)}, u32[]{:S(2)}) async-start(bf16[64,12,512]{2,1,0:T(8,128)(2,1)} %reshape.38), calls=%async_computation.1 | async-start | bytes 2097152 | tf_op jit(solution)/shard_map/all_to_all | solution.py:160
  63.8 1.0 copy-start.23
  64.7 1.0 copy-start.27
  65.7 1.1 copy-start.30
  66.9 1.1 copy-start.33
  77.5 17.1 %copy-start.37 = (bf16[512,3,16]{0,2,1:T(8,128)(2,1)S(1)}, bf16[512,3,16]{0,2,1:T(8,128)(2,1)}, u32[]{:S(2)}) copy-start(bf16[512,3,16]{0,2,1:T(8,128)(2,1)} %copy-done.36) | copy-start | bytes 147460
  78.7 16.2 %copy-start.38 = (bf16[768,48]{0,1:T(8,128)(2,1)S(1)}, bf16[768,48]{0,1:T(8,128)(2,1)}, u32[]{:S(2)}) copy-start(bf16[768,48]{0,1:T(8,128)(2,1)} %param.7) | copy-start | bytes 221188
  82.0 41.6 %all-to-all-start = ((bf16[64,12,512]{2,1,0:T(8,128)(2,1)}), bf16[64,12,512]{2,1,0:T(8,128)(2,1)}, u32[]{:S(2)}, u32[]{:S(2)}) async-start(bf16[64,12,512]{2,1,0:T(8,128)(2,1)} %reshape.37), calls=%async_computation | async-start | bytes 2097152 | tf_op jit(solution)/shard_map/all_to_all | solution.py:160
  87.8 15.0 %collective-permute-start.3 = (bf16[512,128]{1,0:T(8,128)(2,1)}, bf16[512,128]{1,0:T(8,128)(2,1)S(1)}, u32[]{:S(2)}, u32[]{:S(2)}) collective-permute-start(bf16[512,128]{1,0:T(8,128)(2,1)} %get-tuple-element.27), channel_id=1, source_target_pairs={{0,63},{1,0},{2,1},{3,2},{4,3},{5,4},{6,5},{7,6},{8,7},{9,8},{10,9... | collective-permute-start | bytes 393224 | tf_op jit(solution)/shard_map/ppermute | solution.py:26
  88.4 15.8 %collective-permute-start.2 = (bf16[512,128]{1,0:T(8,128)(2,1)}, bf16[512,128]{1,0:T(8,128)(2,1)S(1)}, u32[]{:S(2)}, u32[]{:S(2)}) collective-permute-start(bf16[512,128]{1,0:T(8,128)(2,1)} %get-tuple-element.26), channel_id=1, source_target_pairs={{0,63},{1,0},{2,1},{3,2},{4,3},{5,4},{6,5},{7,6},{8,7},{9,8},{10,9... | collective-permute-start | bytes 393224 | tf_op jit(solution)/shard_map/ppermute | solution.py:26
  94.2 11.5 %collective-permute-start.1 = (bf16[512,128]{1,0:T(8,128)(2,1)}, bf16[512,128]{1,0:T(8,128)(2,1)S(1)}, u32[]{:S(2)}, u32[]{:S(2)}) collective-permute-start(bf16[512,128]{1,0:T(8,128)(2,1)} %get-tuple-element.25), channel_id=1, source_target_pairs={{0,63},{1,0},{2,1},{3,2},{4,3},{5,4},{6,5},{7,6},{8,7},{9,8},{10,9... | collective-permute-start | bytes 393224 | tf_op jit(solution)/shard_map/ppermute | solution.py:26
  106.3 1.5 copy-start.1
  107.8 0.9 copy-start.3
  108.8 0.9 copy-start.5
  109.7 0.9 copy-start.7
  123.5 26.2 %all-to-all-start.3 = ((bf16[64,12,512]{2,1,0:T(8,128)(2,1)}), bf16[64,12,512]{2,1,0:T(8,128)(2,1)S(1)}, u32[]{:S(2)}, u32[]{:S(2)}) async-start(bf16[64,12,512]{2,1,0:T(8,128)(2,1)} %reshape.40), calls=%async_computation.3 | async-start | bytes 2097152 | tf_op jit(solution)/shard_map/all_to_all | solution.py:160
  (16 other events, 12.2 us)
